TPU v7x, 32 devices: a whole 2x2x4 slice. The times are simulated.
32 devices in a mesh: groups: 2 (over y), tok: 8 (over z, x), ch: 2 (over core).
Axes of the slice: x: 2, y: 2, z: 4, core: 2. Of those that a mesh axis runs over, the one named last changes fastest.
Arguments:
- fields: bfloat16 [4096, 512], P(('groups', 'tok'), 'ch'), parts along dimension 0, may hold values from -55 to 55
- cotangent: bfloat16 [4096, 512], P(('groups', 'tok'), 'ch'), parts along dimension 0, may hold values from -6 to 6
- labels: int32 [4096], P(('groups', 'tok')), parts along dimension 0, may hold values from 0 to 511
- reward_masks: int32 [6, 4096], P(None, ('groups', 'tok')), parts along dimension 1, may hold values 0 or 1
- cat_weight: float32 [512], replicated, may hold values from 0.25 to 4
- var_weight: float32 [6], replicated, may hold values from 0.2 to 2
- qkv_weight: bfloat16 [3, 512, 512], P(None, None, 'ch'), may hold values from -0.25 to 0.25
- out_weight: bfloat16 [512, 512], P('ch'), may hold values from -0.25 to 0.25
Outputs:
- grad_fields: bfloat16 [4096, 512], P(('groups', 'tok'), 'ch'), parts along dimension 0
- grad_qkv_weight: float32 [6, 512, 512], P('groups', None, 'ch'), parts along dimension 0
- grad_out_weight: float32 [1024, 512], P(('groups', 'ch')), parts along dimension 0
There are 2 independent parts, one for each index of `groups`. A program takes and returns all parts, laid end to end along the dimension named above; an argument that names none is the same for every part. Nothing has to cross between parts.
All inputs are finite; a program needn't handle non-finite values. No bound on the sum of `reward_masks` on one device may be relied on, other than what follows from the above.
Results may differ from a plain program's by a relative error of at most 0.012.
Values may be sent and summed in bfloat16 or wider, within the bound.
A program may use at most 64 MiB of HBM per device.

v0:
```python
import jax
import jax.numpy as jnp
from jax import lax
from jax.sharding import PartitionSpec as P

D = 512
HEADS = 32


def token_weight(labels, reward_masks, cat_weight, var_weight):
    classes = lax.broadcasted_iota(jnp.int32, (1, cat_weight.shape[0]), 1)
    picked = jnp.sum(jnp.where(labels[:, None] == classes, cat_weight[None, :], 0.0), axis=1)
    reward_boost = 1.0 + jnp.einsum("v,vn->n", var_weight, reward_masks.astype(jnp.float32))
    return picked * reward_boost


def grid_send(array, spread):
    token_count, channels = array.shape
    per_peer = token_count // spread
    return (
        array.reshape(per_peer, spread, channels)
        .transpose(1, 0, 2)
        .reshape(spread, per_peer * channels)
    )


def grid_arrive(array, token_count, channels):
    group_count = token_count // 64
    shaped = array.reshape(64, group_count, channels)
    return shaped.transpose(1, 0, 2).reshape(token_count, channels)


def token_send(array, spread):
    token_count, channels = array.shape
    group_count = token_count // 64
    shaped = array.reshape(group_count, 64, channels).transpose(1, 0, 2)
    return shaped.reshape(spread, token_count // spread * channels)


def token_arrive(array, spread, channels):
    per_peer = array.shape[1] // channels
    shaped = array.reshape(spread, per_peer, channels).transpose(1, 0, 2)
    return shaped.reshape(spread * per_peer, channels)


def widen_channels(fields_own, grad_own):
    return (
        lax.all_gather(fields_own, "ch", axis=1, tiled=True),
        lax.all_gather(grad_own, "ch", axis=1, tiled=True),
    )


def normalize(fields_full):
    values = fields_full.astype(jnp.float32)
    centered = values - jnp.mean(values, axis=1, keepdims=True)
    inv_std = lax.rsqrt(jnp.mean(centered * centered, axis=1, keepdims=True) + 1e-05)
    return (centered * inv_std, inv_std)


def project(normed, grad_full, qkv_weight, out_weight):
    token_count = normed.shape[0]
    projected = jnp.einsum(
        "nc,jcd->njd", normed, qkv_weight, preferred_element_type=jnp.float32
    ).astype(jnp.bfloat16)
    grad_out = jnp.einsum(
        "nc,dc->nd", grad_full, out_weight, preferred_element_type=jnp.float32
    ).astype(jnp.bfloat16)
    return (projected.reshape(token_count, -1), grad_out)


def attend_back(projected, grad_out):
    token_count, channels = grad_out.shape
    head_dim = D // HEADS
    local_heads = channels // head_dim
    groups = token_count // 64
    softmax_scale = head_dim ** (-0.5)
    pieces = projected.reshape(groups, 64, 3, local_heads, head_dim)
    queries = pieces[:, :, 0]
    key_rows = pieces[:, :, 1]
    value_rows = pieces[:, :, 2]
    grad_heads = grad_out.reshape(groups, 64, local_heads, head_dim)
    scores = (
        jnp.einsum("gqhd,gkhd->gqhk", queries, key_rows, preferred_element_type=jnp.float32)
        * softmax_scale
    )
    exponent = jnp.exp(scores)
    attn_probs = exponent / jnp.sum(exponent, axis=3, keepdims=True)
    probs_low = attn_probs.astype(jnp.bfloat16)
    attended = jnp.einsum(
        "gqhk,gkhd->gqhd", probs_low, value_rows, preferred_element_type=jnp.float32
    ).astype(jnp.bfloat16)
    grad_p = jnp.einsum(
        "gqhd,gkhd->gqhk", grad_heads, value_rows, preferred_element_type=jnp.float32
    )
    grad_scores = attn_probs * (grad_p - jnp.sum(attn_probs * grad_p, axis=3, keepdims=True))
    grad_low = grad_scores.astype(jnp.bfloat16)
    grad_q = (
        jnp.einsum("gqhk,gkhd->gqhd", grad_low, key_rows, preferred_element_type=jnp.float32)
        * softmax_scale
    )
    grad_k = (
        jnp.einsum("gqhk,gqhd->gkhd", grad_low, queries, preferred_element_type=jnp.float32)
        * softmax_scale
    )
    grad_v = jnp.einsum(
        "gqhk,gqhd->gkhd", probs_low, grad_heads, preferred_element_type=jnp.float32
    )
    grad_proj = jnp.stack([grad_q, grad_k, grad_v], axis=2).astype(jnp.bfloat16)
    return (attended.reshape(token_count, channels), grad_proj.reshape(token_count, 3 * channels))


def weight_sums(normed, grad_full, attended, grad_proj):
    token_count = normed.shape[0]
    grad_qkv_term = jnp.einsum(
        "nc,njd->jcd",
        normed,
        grad_proj.reshape(token_count, 3, -1),
        preferred_element_type=jnp.float32,
    )
    grad_out_term = jnp.einsum("nd,nc->dc", attended, grad_full, preferred_element_type=jnp.float32)
    return lax.psum((grad_qkv_term, grad_out_term), "tok")


def input_grad(grad_proj, qkv_weight, unit_fields, inv_std, grad_own):
    token_count, channels = grad_own.shape
    partial_value = jnp.einsum(
        "njd,jcd->nc",
        grad_proj.reshape(token_count, 3, channels),
        qkv_weight,
        preferred_element_type=jnp.float32,
    )
    dense_grad = lax.psum(partial_value.astype(jnp.bfloat16), "ch").astype(jnp.float32)
    mean_grad = jnp.mean(dense_grad, axis=1, keepdims=True)
    second = jnp.mean(dense_grad * unit_fields, axis=1, keepdims=True)
    offset = lax.axis_index("ch") * channels
    own_dense = lax.dynamic_slice_in_dim(dense_grad, offset, channels, 1)
    own_unit = lax.dynamic_slice_in_dim(unit_fields, offset, channels, 1)
    return (
        grad_own.astype(jnp.float32) + inv_std * (own_dense - mean_grad - own_unit * second)
    ).astype(jnp.bfloat16)


def shards(fields, cotangent, labels, reward_masks, cat_weight, var_weight, qkv_weight, out_weight):
    token_count, channels = fields.shape
    spread = lax.axis_size("tok")
    weight = token_weight(labels, reward_masks, cat_weight, var_weight)
    weighted = (cotangent.astype(jnp.float32) * weight[:, None]).astype(jnp.bfloat16)
    arrived = (
        lax.all_to_all(grid_send(fields, spread), "tok", split_axis=0, concat_axis=0, tiled=True),
        lax.all_to_all(grid_send(weighted, spread), "tok", split_axis=0, concat_axis=0, tiled=True),
    )
    fields_own = grid_arrive(arrived[0], token_count, channels)
    grad_own = grid_arrive(arrived[1], token_count, channels)
    fields_full, grad_full = widen_channels(fields_own, grad_own)
    unit_fields, inv_std = normalize(fields_full)
    normed = unit_fields.astype(jnp.bfloat16)
    projected, grad_out = project(normed, grad_full, qkv_weight, out_weight)
    attended, grad_proj = attend_back(projected, grad_out)
    grad_qkv_weight, grad_out_weight = weight_sums(normed, grad_full, attended, grad_proj)
    grad_grid = input_grad(grad_proj, qkv_weight, unit_fields, inv_std, grad_own)
    restored = lax.all_to_all(
        token_send(grad_grid, spread), "tok", split_axis=0, concat_axis=0, tiled=True
    )
    grad_fields = token_arrive(restored, spread, channels)
    return (grad_fields, grad_qkv_weight, grad_out_weight)


def solution(mesh):
    return jax.shard_map(
        shards,
        mesh=mesh,
        in_specs=(
            P(("groups", "tok"), "ch"),
            P(("groups", "tok"), "ch"),
            P(("groups", "tok")),
            P(None, ("groups", "tok")),
            P(),
            P(),
            P(None, None, "ch"),
            P("ch", None),
        ),
        out_specs=(P(("groups", "tok"), "ch"), P("groups", None, "ch"), P(("groups", "ch"), None)),
        check_vma=False,
    )
```

profile of v0, /device:TPU:0, one launch (start us, length us, event | category | flops | bytes accessed | tf_op | source)
XLA Modules:
  0.0 186.5 jit_solution(15555083310766638662)
XLA Ops:
  7.2 1.0 select_reduce_fusion
  8.1 0.8 fusion.24
  9.0 1.0 fusion.21
  10.1 0.5 broadcast.56
  10.6 1.4 reduce.3
  12.0 0.7 reshape.108
  12.8 7.3 %all-to-all-start = ((bf16[8,2,4096]{2,1,0:T(2,128)(2,1)}), bf16[8,2,4096]{2,1,0:T(2,128)(2,1)S(1)}, u32[]{:S(2)}, u32[]{:S(2)}) async-start(bf16[8,2,4096]{2,1,0:T(2,128)(2,1)} %reshape.108), calls=%async_computation | async-start | bytes 262144 | tf_op jit(solution)/shard_map/all_to_all | solution.py:150
  20.0 0.9 copy.169
  21.0 1.4 reduce.4
  22.4 0.7 reshape.106
  23.1 4.2 %all-to-all-done = bf16[8,2,4096]{2,1,0:T(2,128)(2,1)S(1)} async-done(((bf16[8,2,4096]{2,1,0:T(2,128)(2,1)}), bf16[8,2,4096]{2,1,0:T(2,128)(2,1)S(1)}, u32[]{:S(2)}, u32[]{:S(2)}) %all-to-all-start) | async-done | bytes 131104 | tf_op jit(solution)/shard_map/all_to_all | solution.py:150
  27.4 3.4 %all-to-all-start.1 = ((bf16[8,2,4096]{2,1,0:T(2,128)(2,1)}), bf16[8,2,4096]{2,1,0:T(2,128)(2,1)S(1)}, u32[]{:S(2)}, u32[]{:S(2)}) async-start(bf16[8,2,4096]{2,1,0:T(2,128)(2,1)} %reshape.106), calls=%async_computation.1 | async-start | bytes 262144 | tf_op jit(solution)/shard_map/all_to_all | solution.py:149
  30.8 0.1 reshape.109
  30.9 0.8 reduce
  31.8 2.0 %all_gather.7 = bf16[256,512]{1,0:T(8,128)(2,1)S(1)} all-gather(bf16[256,256]{1,0:T(8,128)(2,1)S(1)} %bitcast.120), channel_id=1, replica_groups=mesh['groups'=2,'tok'=8,'ch'=2] {'ch'}, dimensions={1}, use_global_device_ids=true | all-gather | bytes 393216 | tf_op jit(solution)/shard_map/all_gather | solution.py:49
  33.8 0.3 convolution_convert_fusion.3
  34.1 0.1 copy.112
  34.2 0.2 reshape.94
  34.3 3.7 %all-to-all-done.1 = bf16[8,2,4096]{2,1,0:T(2,128)(2,1)S(1)} async-done(((bf16[8,2,4096]{2,1,0:T(2,128)(2,1)}), bf16[8,2,4096]{2,1,0:T(2,128)(2,1)S(1)}, u32[]{:S(2)}, u32[]{:S(2)}) %all-to-all-start.1) | async-done | bytes 131104 | tf_op jit(solution)/shard_map/all_to_all | solution.py:149
  38.0 0.1 reshape.107
  38.2 0.8 reduce.1
  39.0 2.0 %all_gather.6 = bf16[256,512]{1,0:T(8,128)(2,1)S(1)} all-gather(bf16[256,256]{1,0:T(8,128)(2,1)S(1)} %bitcast.122), channel_id=1, replica_groups=mesh['groups'=2,'tok'=8,'ch'=2] {'ch'}, dimensions={1}, use_global_device_ids=true | all-gather | bytes 393216 | tf_op jit(solution)/shard_map/all_gather | solution.py:48
  41.0 0.1 convert_reduce_fusion
  41.2 0.2 fusion.12
  41.4 0.4 convolution_convert_fusion
  41.8 0.2 copy.108
  42.0 0.3 reshape_reshape.2
  42.3 0.3 fusion.32
  42.7 0.7 bitcast_reduce_fusion
  43.3 0.7 fusion.6
  44.0 0.8 fusion
  44.8 0.7 fusion.2
  45.5 0.6 fusion.8
  46.2 0.4 fusion.9
  46.6 0.5 fusion.7
  47.0 0.2 copy.120
  47.3 0.2 stack.14
  47.5 0.1 copy.123
  47.6 0.2 copy.117
  47.8 0.2 stack.13
  48.0 0.1 copy.122
  48.1 0.2 copy.115
  48.3 0.2 stack.12
  48.5 0.1 copy.121
  48.7 1.1 fusion.5
  49.8 0.2 all-reduce.6.cloned.1.call-start
  50.0 0.2 copy.129
  50.2 0.2 reshape.98
  50.4 1.0 fusion.35
  51.5 1.6 convolution_bitcast_fusion
  53.1 12.8 %all-reduce.4.cloned.1.call-done = bf16[256,512]{1,0:T(8,128)(2,1)} async-done(((bf16[256,512]{1,0:T(8,128)(2,1)}), bf16[256,512]{1,0:T(8,128)(2,1)}) %all-reduce.4.cloned.1.call-update) | async-done | bytes 262160 | tf_op jit(solution)/shard_map/psum | solution.py:132
  66.0 1.0 convert_element_type.58
  67.0 1.2 convert_reduce_fusion.1
  68.2 0.2 add_convert_fusion
  68.4 0.1 copy.168
  68.6 1.4 reduce.5
  70.0 0.1 reshape.110
  70.0 15.7 %all_to_all.30 = bf16[8,2,4096]{2,1,0:T(2,128)(2,1)S(1)} all-to-all(bf16[8,2,4096]{2,1,0:T(2,128)(2,1)S(1)} %reshape.110), channel_id=1, replica_groups=mesh['groups'=2,'tok'=8,'ch'=2] {'tok'}, dimensions={0} | all-to-all | bytes 262144 | tf_op jit(solution)/shard_map/all_to_all | solution.py:161
  85.8 0.1 reshape.111
  85.9 0.8 reduce.2
  86.7 0.7 copy.167
  87.4 88.4 %all-reduce.6.cloned.1.call-done = (f32[3,512,256]{1,2,0:T(8,128)}, f32[256,512]{1,0:T(8,128)}) async-done(((f32[3,512,256]{1,2,0:T(8,128)}, f32[256,512]{1,0:T(8,128)}), (f32[3,512,256]{1,2,0:T(8,128)}, f32[256,512]{1,0:T(8,128)})) %all-reduce.6.cloned.1.call-update) | async-done | bytes 2097168 | tf_op jit(solution)/shard_map/psum | solution.py:121
  175.8 3.1 %copy.130 = f32[3,512,256]{2,1,0:T(8,128)} copy(f32[3,512,256]{1,2,0:T(8,128)} %get-tuple-element.20) | data formatting | bytes 3145728
  178.9 0.8 copy.174
  (22 shorter events, 0.5 us)
Async XLA Ops:
  7.2 34.2 %copy-start = (bf16[3,512,256]{2,1,0:T(8,128)(2,1)S(1)}, bf16[3,512,256]{2,1,0:T(8,128)(2,1)}, u32[]{:S(2)}) copy-start(bf16[3,512,256]{2,1,0:T(8,128)(2,1)} %param.14) | copy-start | bytes 2359300
  10.6 23.2 %copy-start.2 = (bf16[256,512]{1,0:T(8,128)(2,1)S(1)}, bf16[256,512]{1,0:T(8,128)(2,1)}, u32[]{:S(2)}) copy-start(bf16[256,512]{1,0:T(8,128)(2,1)} %param.15) | copy-start | bytes 786436
  12.8 14.6 %all-to-all-start = ((bf16[8,2,4096]{2,1,0:T(2,128)(2,1)}), bf16[8,2,4096]{2,1,0:T(2,128)(2,1)S(1)}, u32[]{:S(2)}, u32[]{:S(2)}) async-start(bf16[8,2,4096]{2,1,0:T(2,128)(2,1)} %reshape.108), calls=%async_computation | async-start | bytes 262144 | tf_op jit(solution)/shard_map/all_to_all | solution.py:150
  27.4 10.7 %all-to-all-start.1 = ((bf16[8,2,4096]{2,1,0:T(2,128)(2,1)}), bf16[8,2,4096]{2,1,0:T(2,128)(2,1)S(1)}, u32[]{:S(2)}, u32[]{:S(2)}) async-start(bf16[8,2,4096]{2,1,0:T(2,128)(2,1)} %reshape.106), calls=%async_computation.1 | async-start | bytes 262144 | tf_op jit(solution)/shard_map/all_to_all | solution.py:149
  30.7 35.2 %all-reduce.4.cloned.1.call-start = ((), (), s32[]{:S(2)}) async-start(), calls=%async_computation.3 | async-start | bytes 524288 | tf_op jit(solution)/shard_map/psum | solution.py:132
  49.8 126.0 %all-reduce.6.cloned.1.call-start = ((), (), s32[]{:S(2)}) async-start(), calls=%async_computation.4 | async-start | bytes 4194304 | tf_op jit(solution)/shard_map/psum | solution.py:121
  175.8 3.1 %copy-start.1 = (f32[256,512]{1,0:T(8,128)S(1)}, f32[256,512]{1,0:T(8,128)}, u32[]{:S(2)}) copy-start(f32[256,512]{1,0:T(8,128)} %get-tuple-element.34) | copy-start | bytes 1572868
Sparse Core Ops, SparseCore 0:
  49.9 16.0 all-reduce.3
  70.7 105.0 all-reduce.5
where the time goes:
time: 187 us
  waiting for transfers between devices  109 us (58%)
  blocking collectives  19.7 us (11%)
  between operations  14.4 us (8%)
  other arithmetic  11.9 us (6%)
  local copies, waits for them, and re-layouts  11.5 us (6%)
  starting transfers between devices  10.9 us (6%)
  matrix products  8.94 us (5%)
    psum x1, waiting for transfers between devices, weight_sums(): return lax.psum((grad_qkv_term, grad_out_term), 'tok')  88.4 us
    all_to_all x1, blocking collectives, shards(): lax.all_to_all(token_send(grad_grid, spread), 'tok', split_axis=0, concat...  15.7 us
    psum x1, waiting for transfers between devices, input_grad(): lax.psum(partial_value.astype(jnp.bfloat16), 'ch').astype(jnp.float32)  12.8 us
    all_to_all x1, starting transfers between devices, shards(): lax.all_to_all(grid_send(weighted, spread), 'tok', split_axis=0, concat_a...  7.25 us
    unnamed x15, local copies, waits for them, and re-layouts  5.82 us
    all_to_all x1, waiting for transfers between devices, shards(): lax.all_to_all(grid_send(weighted, spread), 'tok', split_axis=0, concat_a...  4.24 us
  transfers between devices with their start and end apart: 4, of which 4 were waited for; matrix products, arithmetic and copies ran while one was open for 7% of the time, Pallas kernels for 0%

commit v1 on v0

v1 whole, which is shorter than its diff:
```python
import functools

import jax
import jax.numpy as jnp
from jax import lax
from jax.experimental import pallas as pl
from jax.experimental.pallas import tpu as pltpu
from jax.sharding import PartitionSpec as P

HEAD_DIM = 16
MEMBERS = 64
F32 = jnp.float32
BF16 = jnp.bfloat16
MESH = pl.DeviceIdType.MESH


def nn(a, b):
    return lax.dot_general(a, b, (((1,), (0,)), ((), ())), preferred_element_type=F32)


def nt(a, b):
    return lax.dot_general(a, b, (((1,), (1,)), ((), ())), preferred_element_type=F32)


def tn(a, b):
    return lax.dot_general(a, b, (((0,), (0,)), ((), ())), preferred_element_type=F32)


def iota(shape, dim):
    return lax.broadcasted_iota(jnp.int32, shape, dim)


def repeat(start, stop, body):
    if stop - start <= 8:
        for k in range(start, stop):
            body(k)
    else:
        lax.fori_loop(start, stop, lambda k, _: (body(k), 0)[1], 0)


def spread_matrix(tokens, spread, rows, slots, transposed):
    shape = (tokens, spread * slots) if transposed else (spread * slots, tokens)
    slot, token = (1, 0) if transposed else (0, 1)
    slot, token = iota(shape, slot), iota(shape, token)
    peer, place = slot // slots, slot % slots
    hit = (token == place * spread + peer) & (place < rows)
    return jnp.where(hit, 1.0, 0.0).astype(BF16)


def group_matrix(tokens, spread, rows, slots, transposed):
    shape = (spread * slots, tokens) if transposed else (tokens, spread * slots)
    token, slot = (1, 0) if transposed else (0, 1)
    token, slot = iota(shape, token), iota(shape, slot)
    groups = tokens // MEMBERS
    source = (token % MEMBERS) * groups + token // MEMBERS
    peer, place = slot // slots, slot % slots
    hit = (source == peer * rows + place) & (place < rows)
    return jnp.where(hit, 1.0, 0.0).astype(BF16)


def split_sum(values, ones):
    high = values.astype(BF16)
    low = (values - high.astype(F32)).astype(BF16)
    return nn(high, ones) + nn(low, ones)


def attend(q, k, v, g):
    channels = q.shape[1]
    per = 256 // MEMBERS
    wide = per * MEMBERS
    scale = HEAD_DIM ** (-0.5)
    row_head = iota((wide, channels), 0) // MEMBERS
    col_head = iota((wide, channels), 1) // HEAD_DIM
    ones = iota((wide, wide), 0) // MEMBERS == iota((wide, wide), 1) // MEMBERS
    ones = jnp.where(ones, 1.0, 0.0).astype(BF16)
    k_all = jnp.concatenate([k] * per, axis=0)
    v_all = jnp.concatenate([v] * per, axis=0)
    attended = grad_q = grad_k = grad_v = None
    for chunk in range(channels // HEAD_DIM // per):
        own = row_head + chunk * per == col_head
        keep = jnp.where(own, 1.0, 0.0).astype(BF16)
        k_wide = k_all * keep
        v_wide = v_all * keep
        exponent = jnp.exp(nt(q, k_wide) * scale)
        probs = exponent / split_sum(exponent, ones)
        low = probs.astype(BF16)
        grad_p = nt(g, v_wide)
        grad_scores = probs * (grad_p - split_sum(probs * grad_p, ones))
        grad_low = grad_scores.astype(BF16)
        terms = [nn(low, v_wide), nn(grad_low, k_wide)]
        for left, right in ((grad_low, q), (low, g)):
            full = jnp.where(own, tn(left, right), 0.0)
            part = full[:MEMBERS]
            for h in range(1, per):
                part = part + full[h * MEMBERS:(h + 1) * MEMBERS]
            terms.append(part)
        if chunk == 0:
            attended, grad_q, grad_k, grad_v = terms
        else:
            attended, grad_q = attended + terms[0], grad_q + terms[1]
            grad_k, grad_v = grad_k + terms[2], grad_v + terms[3]
    return (
        attended.astype(BF16),
        (grad_q * scale).astype(BF16),
        (grad_k * scale).astype(BF16),
        grad_v.astype(BF16),
    )


def kernel(
    spread,
    fields,
    cotangent,
    labels,
    masks,
    cat_weight,
    var_weight,
    qkv_weight,
    out_weight,
    out_fields,
    sums,
    send,
    got,
    dense_send,
    dense_got,
    back_send,
    back_got,
    terms,
    from_x,
    pair,
    from_z,
    stack,
    in_send,
    in_recv,
    fw_send,
    fw_recv,
    de_send,
    de_recv,
    bk_send,
    bk_recv,
    x_send,
    x_recv,
    z_send,
    z_recv,
    gz_send,
    gz_recv,
    gx_send,
    gx_recv,
):
    me = lax.axis_index("tok")
    ch = lax.axis_index("ch")
    x, z = lax.rem(me, 2), me // 2
    partner = 2 * z + 1 - x
    tokens, channels = fields.shape
    rows = tokens // spread
    slots = send.shape[1]
    parts, _, depth, block, _ = terms.shape

    def remote(src, dst, send_sem, recv_sem, where):
        return pltpu.make_async_remote_copy(
            src_ref=src, dst_ref=dst, send_sem=send_sem, recv_sem=recv_sem,
            device_id=where, device_id_type=MESH,
        )

    barrier = pltpu.get_barrier_semaphore()

    def greet(k):
        pl.semaphore_signal(
            barrier, inc=1, device_id={"tok": lax.rem(me + k, spread)}, device_id_type=MESH
        )

    repeat(1, spread, greet)
    pl.semaphore_signal(barrier, inc=1, device_id={"ch": 1 - ch}, device_id_type=MESH)

    classes = cat_weight.shape[1]
    onehot = jnp.where(iota((classes, tokens), 0) == labels[...], 1.0, 0.0).astype(BF16)
    left = jnp.broadcast_to(cat_weight[...], (16, classes))
    picked = jnp.zeros((16, tokens), F32)
    for _ in range(3):
        piece = left.astype(BF16)
        picked = picked + nn(piece, onehot)
        left = left - piece.astype(F32)
    boost = jnp.ones((1, tokens), F32)
    seen = masks[...].astype(F32)
    for variable in range(masks.shape[0]):
        boost = boost + var_weight[variable] * seen[variable:variable + 1]
    weight_row = picked[:1] * boost
    diagonal = iota((tokens, tokens), 0) == iota((tokens, tokens), 1)
    weight = jnp.sum(jnp.where(diagonal, weight_row, 0.0), axis=1, keepdims=True)
    weighted = (cotangent[...].astype(F32) * weight).astype(BF16)
    order = spread_matrix(tokens, spread, rows, slots, False)
    send[:, :, :channels] = nn(order, fields[...]).astype(BF16).reshape(spread, slots, channels)
    send[:, :, channels:] = nn(order, weighted).astype(BF16).reshape(spread, slots, channels)

    pl.semaphore_wait(barrier, spread)

    def to_peer(k):
        peer = lax.rem(me + k, spread)
        return remote(
            send.at[peer], got.at[ch, me], in_send.at[peer], in_recv.at[me], {"tok": peer}
        )

    def from_peer(k):
        peer = lax.rem(me + spread - k, spread)
        return peer, remote(
            send.at[peer], got.at[ch, peer], in_send.at[peer], in_recv.at[peer], {"tok": peer}
        )

    def forward(peer):
        return remote(
            got.at[ch, peer], got.at[ch, peer], fw_send.at[peer], fw_recv.at[peer], {"ch": 1 - ch}
        )

    def sibling(peer):
        return remote(
            got.at[1 - ch, peer], got.at[1 - ch, peer], fw_send.at[peer], fw_recv.at[peer],
            {"ch": 1 - ch},
        )

    repeat(1, spread, lambda k: to_peer(k).start())
    got[ch, me] = send[me]
    forward(me).start()

    def pass_on(k):
        peer, copy = from_peer(k)
        copy.wait_recv()
        forward(peer).start()

    repeat(1, spread, pass_on)
    repeat(0, spread, lambda k: sibling(k).wait_recv())

    place = group_matrix(tokens, spread, rows, slots, False)
    low = nn(place, got[0].reshape(spread * slots, 2 * channels))
    high = nn(place, got[1].reshape(spread * slots, 2 * channels))
    values = jnp.concatenate([low[:, :channels], high[:, :channels]], axis=1)
    grad_full = jnp.concatenate([low[:, channels:], high[:, channels:]], axis=1).astype(BF16)
    centered = values - jnp.mean(values, axis=1, keepdims=True)
    inv_std = lax.rsqrt(jnp.mean(centered * centered, axis=1, keepdims=True) + 1e-05)
    unit = centered * inv_std
    normed = unit.astype(BF16)
    q = nn(normed, qkv_weight[0]).astype(BF16)
    k = nn(normed, qkv_weight[1]).astype(BF16)
    v = nn(normed, qkv_weight[2]).astype(BF16)
    g = nt(grad_full, out_weight[...]).astype(BF16)
    for group in range(tokens // MEMBERS):
        rows_of = slice(group * MEMBERS, (group + 1) * MEMBERS)
        results = attend(q[rows_of], k[rows_of], v[rows_of], g[rows_of])
        for index, result in enumerate(results):
            stack[index, rows_of] = result

    def to_partner(part):
        return remote(
            terms.at[part, 1 - x], from_x.at[part], x_send.at[part], x_recv.at[part],
            {"tok": partner},
        )

    def store_terms(index, value):
        value = value.astype(BF16)
        if parts == 4:
            terms[index] = value.reshape(2, depth, block, 256)
        else:
            half = depth // 2
            first = (index % 2) * half
            terms[0, index // 2, first:first + half] = value.reshape(half, block, 256)

    turned = normed.astype(F32).T.astype(BF16)
    out_term = tn(stack[0], grad_full)
    store_terms(3, jnp.concatenate([out_term[:, :256], out_term[:, 256:]], axis=0))
    if parts == 4:
        to_partner(3).start()
    for index in range(3):
        store_terms(index, nn(turned, stack[1 + index]))
        if parts == 4:
            to_partner(index).start()
    if parts == 1:
        to_partner(0).start()
    sequence = (3, 0, 1, 2) if parts == 4 else (0,)

    dense = nt(stack[1], qkv_weight[0]) + nt(stack[2], qkv_weight[1]) + nt(stack[3], qkv_weight[2])
    dense_send[...] = dense.astype(BF16)
    dense_copy = remote(dense_send, dense_got, de_send, de_recv, {"ch": 1 - ch})
    dense_copy.start()

    def to_z(part, step):
        there = lax.rem(z + step, depth)
        return remote(
            pair.at[part, there], from_z.at[part, z],
            z_send.at[part, there], z_recv.at[part, z], {"tok": 2 * there + x},
        )

    def from_z_peer(part, step):
        there = lax.rem(z + step, depth)
        return there, remote(
            pair.at[part, there], from_z.at[part, there],
            z_send.at[part, there], z_recv.at[part, there], {"tok": 2 * there + x},
        )

    def pair_up(part):
        to_partner(part).wait_recv()
        pair[part] = (terms[part, x].astype(F32) + from_x[part].astype(F32)).astype(BF16)
        repeat(1, depth, lambda step: to_z(part, step).start())

    pair_up(sequence[0])

    dense_copy.wait()
    dense = dense_send[...].astype(F32) + dense_got[...].astype(F32)
    mean = jnp.mean(dense, axis=1, keepdims=True)
    second = jnp.mean(dense * unit, axis=1, keepdims=True)
    first_half = ch == 0
    own_dense = jnp.where(first_half, dense[:, :channels], dense[:, channels:])
    own_unit = jnp.where(first_half, unit[:, :channels], unit[:, channels:])
    own_grad = jnp.where(first_half, low[:, channels:], high[:, channels:])
    grad = (own_grad + inv_std * (own_dense - mean - own_unit * second)).astype(BF16)
    place_back = group_matrix(tokens, spread, rows, slots, True)
    back_send[...] = nn(place_back, grad).astype(BF16).reshape(spread, slots, channels)

    def give_back(k):
        peer = lax.rem(me + k, spread)
        return remote(
            back_send.at[peer], back_got.at[me], bk_send.at[peer], bk_recv.at[me], {"tok": peer}
        )

    def take_back(k):
        peer = lax.rem(me + spread - k, spread)
        return remote(
            back_send.at[peer], back_got.at[peer], bk_send.at[peer], bk_recv.at[peer],
            {"tok": peer},
        )

    repeat(1, spread, lambda k: give_back(k).start())
    back_got[me] = back_send[me]

    for part in sequence[1:]:
        pair_up(part)

    def share_z(part, step):
        there = lax.rem(z + step, depth)
        return remote(
            sums.at[part, x, z], sums.at[part, x, z],
            gz_send.at[part, there], gz_recv.at[part, z], {"tok": 2 * there + x},
        )

    def shared_z(part, step):
        there = lax.rem(z + step, depth)
        return there, remote(
            sums.at[part, x, there], sums.at[part, x, there],
            gz_send.at[part, there], gz_recv.at[part, there], {"tok": 2 * there + x},
        )

    def share_x(part, there):
        return remote(
            sums.at[part, x, there], sums.at[part, x, there],
            gx_send.at[part, there], gx_recv.at[part, there], {"tok": partner},
        )

    def shared_x(part, there):
        return remote(
            sums.at[part, 1 - x, there], sums.at[part, 1 - x, there],
            gx_send.at[part, there], gx_recv.at[part, there], {"tok": partner},
        )

    for part in sequence:
        if depth <= 9:
            total = pair[part, z].astype(F32)
            for step in range(1, depth):
                there, copy = from_z_peer(part, step)
                copy.wait_recv()
                total = total + from_z[part, there].astype(F32)
        else:
            def add(step, total):
                there, copy = from_z_peer(part, step)
                copy.wait_recv()
                return total + from_z[part, there].astype(F32)

            total = lax.fori_loop(1, depth, add, pair[part, z].astype(F32))
        sums[part, x, z] = total.astype(BF16)
        repeat(1, depth, lambda step: share_z(part, step).start())
        share_x(part, z).start()

    repeat(1, spread, lambda k: take_back(k).wait_recv())
    order_back = spread_matrix(tokens, spread, rows, slots, True)
    restored = nn(order_back, back_got[...].reshape(spread * slots, channels))
    out_fields[...] = restored.astype(BF16)

    def go_on(part, step):
        there, copy = shared_z(part, step)
        copy.wait_recv()
        share_x(part, there).start()

    for part in sequence:
        repeat(1, depth, lambda step: go_on(part, step))
    for part in sequence:
        repeat(0, depth, lambda there: shared_x(part, there).wait_recv())

    repeat(1, spread, lambda k: to_peer(k).wait_send())
    repeat(0, spread, lambda k: forward(k).wait_send())
    repeat(1, spread, lambda k: give_back(k).wait_send())
    for part in sequence:
        to_partner(part).wait_send()
        repeat(1, depth, lambda step: to_z(part, step).wait_send())
        repeat(1, depth, lambda step: share_z(part, step).wait_send())
        repeat(0, depth, lambda there: share_x(part, there).wait_send())


def shards(fields, cotangent, labels, reward_masks, cat_weight, var_weight, qkv_weight, out_weight):
    tokens, channels = fields.shape
    spread = lax.axis_size("tok")
    slots = max(tokens // spread, 16)
    depth = spread // 2
    width = qkv_weight.shape[1]
    total = 2048
    parts = 4 if total // (4 * spread) >= 16 else 1
    block = total // (parts * spread)
    vmem = pl.BlockSpec(memory_space=pltpu.VMEM)
    smem = pl.BlockSpec(memory_space=pltpu.SMEM)
    dma = pltpu.SemaphoreType.DMA
    grad_fields, sums = pl.pallas_call(
        functools.partial(kernel, spread),
        out_shape=(
            jax.ShapeDtypeStruct((tokens, channels), BF16),
            jax.ShapeDtypeStruct((parts, 2, depth, block, 256), BF16),
        ),
        in_specs=[vmem] * 5 + [smem] + [vmem] * 2,
        out_specs=(vmem, vmem),
        scratch_shapes=[
            pltpu.VMEM((spread, slots, 2 * channels), BF16),
            pltpu.VMEM((2, spread, slots, 2 * channels), BF16),
            pltpu.VMEM((tokens, width), BF16),
            pltpu.VMEM((tokens, width), BF16),
            pltpu.VMEM((spread, slots, channels), BF16),
            pltpu.VMEM((spread, slots, channels), BF16),
            pltpu.VMEM((parts, 2, depth, block, 256), BF16),
            pltpu.VMEM((parts, depth, block, 256), BF16),
            pltpu.VMEM((parts, depth, block, 256), BF16),
            pltpu.VMEM((parts, depth, block, 256), BF16),
            pltpu.VMEM((4, tokens, channels), BF16),
            dma((spread,)), dma((spread,)),
            dma((spread,)), dma((spread,)),
            dma, dma,
            dma((spread,)), dma((spread,)),
            dma((parts,)), dma((parts,)),
            dma((parts, depth)), dma((parts, depth)),
            dma((parts, depth)), dma((parts, depth)),
            dma((parts, depth)), dma((parts, depth)),
        ],
        compiler_params=pltpu.CompilerParams(
            collective_id=0, has_side_effects=True, vmem_limit_bytes=48 * 1024 * 1024
        ),
        cost_estimate=pl.CostEstimate(
            flops=2_000_000_000, bytes_accessed=8_000_000, transcendentals=300_000
        ),
    )(
        fields,
        cotangent,
        labels.reshape(1, tokens),
        reward_masks,
        cat_weight.reshape(1, -1),
        var_weight,
        qkv_weight,
        out_weight,
    )
    sums = sums.reshape(4, 512, 256)
    grad_qkv = sums[:3].astype(F32)
    grad_out = jnp.concatenate([sums[3, :256], sums[3, 256:]], axis=1).astype(F32)
    return grad_fields, grad_qkv, grad_out


def solution(mesh):
    return jax.shard_map(
        shards,
        mesh=mesh,
        in_specs=(
            P(("groups", "tok"), "ch"),
            P(("groups", "tok"), "ch"),
            P(("groups", "tok")),
            P(None, ("groups", "tok")),
            P(),
            P(),
            P(None, None, "ch"),
            P("ch", None),
        ),
        out_specs=(P(("groups", "tok"), "ch"), P("groups", None, "ch"), P(("groups", "ch"), None)),
        check_vma=False,
    )
```

time: 187 us -> 71.2 us (0.38)
  the two profiles are of different devices: /device:TPU:0 before, /device:TPU:26 now
where the time goes in v1:
time: 71.2 us; the launch traced here: 70.9 us
  Pallas kernels  60.8 us (85%)
  local copies, waits for them, and re-layouts  7.32 us (10%)
  other arithmetic  2.18 us (3%)
    pallas_call x1, Pallas kernels, shards(): pl.pallas_call(functools.partial(kernel, spread), out_shape=(jax.ShapeDty...  60.8 us
    unnamed x17, local copies, waits for them, and re-layouts  7.25 us

profile of v1, /device:TPU:26, one launch (start us, length us, event | category | flops | bytes accessed | tf_op | source)
XLA Modules:
  0.0 70.9 jit_solution(18126390943096068803)
XLA Ops:
  0.6 0.0 copy-start
  0.6 1.1 %copy-done = bf16[3,512,256]{2,1,0:T(8,128)(2,1)S(1)} copy-done((bf16[3,512,256]{2,1,0:T(8,128)(2,1)S(1)}, bf16[3,512,256]{2,1,0:T(8,128)(2,1)}, u32[]{:S(2)}) %copy-start) | copy-done | bytes 786456
  1.8 0.0 copy-start.1
  1.8 0.9 %copy-done.1 = bf16[256,512]{1,0:T(8,128)(2,1)S(1)} copy-done((bf16[256,512]{1,0:T(8,128)(2,1)S(1)}, bf16[256,512]{1,0:T(8,128)(2,1)}, u32[]{:S(2)}) %copy-start.1) | copy-done | bytes 262168
  2.7 0.0 copy-start.2
  2.7 0.9 %copy-done.2 = bf16[256,256]{1,0:T(8,128)(2,1)S(1)} copy-done((bf16[256,256]{1,0:T(8,128)(2,1)S(1)}, bf16[256,256]{1,0:T(8,128)(2,1)}, u32[]{:S(2)}) %copy-start.2) | copy-done | bytes 131096
  3.6 0.0 copy-start.3
  3.6 0.9 %copy-done.3 = bf16[256,256]{1,0:T(8,128)(2,1)S(1)} copy-done((bf16[256,256]{1,0:T(8,128)(2,1)S(1)}, bf16[256,256]{1,0:T(8,128)(2,1)}, u32[]{:S(2)}) %copy-start.3) | copy-done | bytes 131096
  4.5 0.0 copy-start.4
  4.5 0.7 copy-done.4
  5.2 0.0 copy-start.5
  5.2 0.7 copy-done.5
  5.9 0.0 copy-start.6
  5.9 0.7 copy-done.6
  6.6 0.0 copy-start.7
  6.6 0.7 copy-done.7
  7.2 60.8 %shard_map.103 = (bf16[256,256]{1,0:T(8,128)(2,1)S(1)}, bf16[4,2,4,64,256]{4,3,2,1,0:T(8,128)(2,1)S(1)}) custom-call(bf16[256,256]{1,0:T(8,128)(2,1)S(1)} %copy-done.2, bf16[256,256]{1,0:T(8,128)(2,1)S(1)} %copy-done.3, s32[1,256]{1,0:T(1,128)S(1)} %bitcast.12, s32[6,256]{1,0:T(8,128)S(1)} %copy-done.4, f32[1,512]{1,0:T(1,128)S(1)} %bitcast.11, ...), custom_call_target="tpu_custom_call" | custom-call | flops 2000000000 | bytes 8000000 | tf_op jit(solution)/shard_map/pallas_call | solution.py:417
  68.0 0.9 %maximum_convert_fusion = f32[256,512]{1,0:T(8,128)} fusion(bf16[256,256]{1,0:T(8,128)(2,1)S(1)} %get-tuple-element.8, bf16[256,256]{1,0:T(8,128)(2,1)S(1)} %get-tuple-element.7), kind=kLoop, calls=%fused_computation.1 | loop fusion | flops 524288 | bytes 786432 | tf_op jit(solution)/shard_map/convert_element_type | solution.py:464
  68.9 0.1 slice.10
  68.9 1.3 %bitcast_convert_fusion = f32[3,512,256]{2,1,0:T(8,128)} fusion(bf16[3,2,4,64,256]{4,3,2,1,0:T(8,128)(2,1)S(1)} %slice.10), kind=kLoop, calls=%fused_computation | loop fusion | flops 393216 | bytes 2359296 | tf_op jit(solution)/shard_map/convert_element_type | solution.py:463
  70.3 0.7 copy.12
  (1 shorter events, 0.0 us)
Async XLA Ops:
  0.6 1.1 %copy-start = (bf16[3,512,256]{2,1,0:T(8,128)(2,1)S(1)}, bf16[3,512,256]{2,1,0:T(8,128)(2,1)}, u32[]{:S(2)}) copy-start(bf16[3,512,256]{2,1,0:T(8,128)(2,1)} %qkv_weight.1) | copy-start | bytes 2359300
  1.8 0.9 %copy-start.1 = (bf16[256,512]{1,0:T(8,128)(2,1)S(1)}, bf16[256,512]{1,0:T(8,128)(2,1)}, u32[]{:S(2)}) copy-start(bf16[256,512]{1,0:T(8,128)(2,1)} %out_weight.1) | copy-start | bytes 786436
  2.7 0.9 %copy-start.2 = (bf16[256,256]{1,0:T(8,128)(2,1)S(1)}, bf16[256,256]{1,0:T(8,128)(2,1)}, u32[]{:S(2)}) copy-start(bf16[256,256]{1,0:T(8,128)(2,1)} %fields.1) | copy-start | bytes 393220
  3.6 0.9 %copy-start.3 = (bf16[256,256]{1,0:T(8,128)(2,1)S(1)}, bf16[256,256]{1,0:T(8,128)(2,1)}, u32[]{:S(2)}) copy-start(bf16[256,256]{1,0:T(8,128)(2,1)} %cotangent.1) | copy-start | bytes 393220
  4.5 0.7 copy-start.4
  5.2 0.7 copy-start.5
  5.9 0.7 copy-start.6
  6.6 0.7 copy-start.7

commit v2 on v1

--- a/solution.py
+++ b/solution.py
@@ -109,16 +109,26 @@
 
 def kernel(
     spread,
+    fields_hbm,
+    cotangent_hbm,
+    labels_hbm,
+    masks_hbm,
+    cat_weight_hbm,
+    var_weight,
+    qkv_weight_hbm,
+    out_weight_hbm,
+    out_fields,
+    out_qkv,
+    out_out,
+    sums,
     fields,
     cotangent,
     labels,
     masks,
     cat_weight,
-    var_weight,
     qkv_weight,
     out_weight,
-    out_fields,
-    sums,
+    load_sem,
     send,
     got,
     dense_send,
@@ -147,6 +157,20 @@
     gx_send,
     gx_recv,
 ):
+    loads = [
+        pltpu.make_async_copy(source, target, load_sem.at[index])
+        for index, (source, target) in enumerate((
+            (labels_hbm, labels),
+            (cat_weight_hbm, cat_weight),
+            (masks_hbm, masks),
+            (fields_hbm, fields),
+            (cotangent_hbm, cotangent),
+            (qkv_weight_hbm, qkv_weight),
+            (out_weight_hbm, out_weight),
+        ))
+    ]
+    for load in loads:
+        load.start()
     me = lax.axis_index("tok")
     ch = lax.axis_index("ch")
     x, z = lax.rem(me, 2), me // 2
@@ -172,6 +196,8 @@
     repeat(1, spread, greet)
     pl.semaphore_signal(barrier, inc=1, device_id={"ch": 1 - ch}, device_id_type=MESH)
 
+    for load in loads[:5]:
+        load.wait()
     classes = cat_weight.shape[1]
     onehot = jnp.where(iota((classes, tokens), 0) == labels[...], 1.0, 0.0).astype(BF16)
     left = jnp.broadcast_to(cat_weight[...], (16, classes))
@@ -229,6 +255,8 @@
     repeat(1, spread, pass_on)
     repeat(0, spread, lambda k: sibling(k).wait_recv())
 
+    for load in loads[5:]:
+        load.wait()
     place = group_matrix(tokens, spread, rows, slots, False)
     low = nn(place, got[0].reshape(spread * slots, 2 * channels))
     high = nn(place, got[1].reshape(spread * slots, 2 * channels))
@@ -242,12 +270,6 @@
     k = nn(normed, qkv_weight[1]).astype(BF16)
     v = nn(normed, qkv_weight[2]).astype(BF16)
     g = nt(grad_full, out_weight[...]).astype(BF16)
-    for group in range(tokens // MEMBERS):
-        rows_of = slice(group * MEMBERS, (group + 1) * MEMBERS)
-        results = attend(q[rows_of], k[rows_of], v[rows_of], g[rows_of])
-        for index, result in enumerate(results):
-            stack[index, rows_of] = result
-
     def to_partner(part):
         return remote(
             terms.at[part, 1 - x], from_x.at[part], x_send.at[part], x_recv.at[part],
@@ -263,23 +285,11 @@
             first = (index % 2) * half
             terms[0, index // 2, first:first + half] = value.reshape(half, block, 256)
 
-    turned = normed.astype(F32).T.astype(BF16)
-    out_term = tn(stack[0], grad_full)
-    store_terms(3, jnp.concatenate([out_term[:, :256], out_term[:, 256:]], axis=0))
-    if parts == 4:
-        to_partner(3).start()
-    for index in range(3):
-        store_terms(index, nn(turned, stack[1 + index]))
+    def part_rows(ref, index):
         if parts == 4:
-            to_partner(index).start()
-    if parts == 1:
-        to_partner(0).start()
-    sequence = (3, 0, 1, 2) if parts == 4 else (0,)
-
-    dense = nt(stack[1], qkv_weight[0]) + nt(stack[2], qkv_weight[1]) + nt(stack[3], qkv_weight[2])
-    dense_send[...] = dense.astype(BF16)
-    dense_copy = remote(dense_send, dense_got, de_send, de_recv, {"ch": 1 - ch})
-    dense_copy.start()
+            return ref[index].reshape(512, 256)
+        first = (index % 2) * (depth // 2)
+        return ref[0, index // 2, first:first + depth // 2].reshape(512, 256)
 
     def to_z(part, step):
         there = lax.rem(z + step, depth)
@@ -300,7 +310,41 @@
         pair[part] = (terms[part, x].astype(F32) + from_x[part].astype(F32)).astype(BF16)
         repeat(1, depth, lambda step: to_z(part, step).start())
 
-    pair_up(sequence[0])
+    turned = normed.astype(F32).T.astype(BF16)
+    groups = tokens // MEMBERS
+    half = channels // 2
+    for h in range(2):
+        cols = slice(h * half, (h + 1) * half)
+        for group in range(groups):
+            rows_of = slice(group * MEMBERS, (group + 1) * MEMBERS)
+            results = attend(
+                q[rows_of, cols], k[rows_of, cols], v[rows_of, cols], g[rows_of, cols]
+            )
+            for index, result in enumerate(results):
+                stack[index, rows_of, cols] = result
+            if h == 1 and parts == 4 and group == groups - 2:
+                pair_up(0)
+        both = jnp.concatenate([stack[1, :, cols], stack[2, :, cols]], axis=1)
+        store_terms(2 * h, nn(turned, both))
+        if parts == 4:
+            to_partner(2 * h).start()
+        out_term = tn(stack[0, :, cols], grad_full)
+        out_term = jnp.concatenate(
+            [out_term[:, j * half:(j + 1) * half] for j in range(4)], axis=0
+        )
+        value_term = nn(turned, stack[3, :, cols])
+        store_terms(2 * h + 1, jnp.concatenate([value_term, out_term], axis=1))
+        if parts == 4:
+            to_partner(2 * h + 1).start()
+    if parts == 1:
+        to_partner(0).start()
+
+    dense = nt(stack[1], qkv_weight[0]) + nt(stack[2], qkv_weight[1]) + nt(stack[3], qkv_weight[2])
+    dense_send[...] = dense.astype(BF16)
+    dense_copy = remote(dense_send, dense_got, de_send, de_recv, {"ch": 1 - ch})
+    dense_copy.start()
+
+    pair_up(1 if parts == 4 else 0)
 
     dense_copy.wait()
     dense = dense_send[...].astype(F32) + dense_got[...].astype(F32)
@@ -330,9 +374,6 @@
     repeat(1, spread, lambda k: give_back(k).start())
     back_got[me] = back_send[me]
 
-    for part in sequence[1:]:
-        pair_up(part)
-
     def share_z(part, step):
         there = lax.rem(z + step, depth)
         return remote(
@@ -359,7 +400,12 @@
             gx_send.at[part, there], gx_recv.at[part, there], {"tok": partner},
         )
 
-    for part in sequence:
+    def go_on(part, step):
+        there, copy = shared_z(part, step)
+        copy.wait_recv()
+        share_x(part, there).start()
+
+    def finish(part):
         if depth <= 9:
             total = pair[part, z].astype(F32)
             for step in range(1, depth):
@@ -377,25 +423,55 @@
         repeat(1, depth, lambda step: share_z(part, step).start())
         share_x(part, z).start()
 
-    repeat(1, spread, lambda k: take_back(k).wait_recv())
-    order_back = spread_matrix(tokens, spread, rows, slots, True)
-    restored = nn(order_back, back_got[...].reshape(spread * slots, channels))
-    out_fields[...] = restored.astype(BF16)
-
-    def go_on(part, step):
-        there, copy = shared_z(part, step)
-        copy.wait_recv()
-        share_x(part, there).start()
-
-    for part in sequence:
+    def restore():
+        repeat(1, spread, lambda k: take_back(k).wait_recv())
+        order_back = spread_matrix(tokens, spread, rows, slots, True)
+        restored = nn(order_back, back_got[...].reshape(spread * slots, channels))
+        out_fields[...] = restored.astype(BF16)
+
+    def pass_over(part):
         repeat(1, depth, lambda step: go_on(part, step))
-    for part in sequence:
+
+    def place_terms(index):
+        block_rows = part_rows(sums, index)
+        h = index // 2
+        cols = slice(h * half, (h + 1) * half)
+        if index % 2 == 0:
+            out_qkv[0, :, cols] = block_rows[:, :half]
+            out_qkv[1, :, cols] = block_rows[:, half:]
+        else:
+            out_qkv[2, :, cols] = block_rows[:, :half]
+            for j in range(4):
+                out_out[cols, j * half:(j + 1) * half] = block_rows[j * half:(j + 1) * half, half:]
+
+    if parts == 4:
+        finish(0)
+        pair_up(2)
+        finish(1)
+        pass_over(0)
+        pair_up(3)
+        finish(2)
+        pass_over(1)
+        restore()
+        finish(3)
+        pass_over(2)
+        pass_over(3)
+    else:
+        finish(0)
+        restore()
+        pass_over(0)
+    for part in range(parts):
         repeat(0, depth, lambda there: shared_x(part, there).wait_recv())
+        if parts == 4:
+            place_terms(part)
+    if parts == 1:
+        for index in range(4):
+            place_terms(index)
 
     repeat(1, spread, lambda k: to_peer(k).wait_send())
     repeat(0, spread, lambda k: forward(k).wait_send())
     repeat(1, spread, lambda k: give_back(k).wait_send())
-    for part in sequence:
+    for part in range(parts):
         to_partner(part).wait_send()
         repeat(1, depth, lambda step: to_z(part, step).wait_send())
         repeat(1, depth, lambda step: share_z(part, step).wait_send())
@@ -412,17 +488,28 @@
     parts = 4 if total // (4 * spread) >= 16 else 1
     block = total // (parts * spread)
     vmem = pl.BlockSpec(memory_space=pltpu.VMEM)
+    hbm = pl.BlockSpec(memory_space=pltpu.HBM)
     smem = pl.BlockSpec(memory_space=pltpu.SMEM)
     dma = pltpu.SemaphoreType.DMA
-    grad_fields, sums = pl.pallas_call(
+    grad_fields, grad_qkv, grad_out = pl.pallas_call(
         functools.partial(kernel, spread),
         out_shape=(
             jax.ShapeDtypeStruct((tokens, channels), BF16),
-            jax.ShapeDtypeStruct((parts, 2, depth, block, 256), BF16),
+            jax.ShapeDtypeStruct(qkv_weight.shape, BF16),
+            jax.ShapeDtypeStruct(out_weight.shape, BF16),
         ),
-        in_specs=[vmem] * 5 + [smem] + [vmem] * 2,
-        out_specs=(vmem, vmem),
+        in_specs=[hbm] * 5 + [smem] + [hbm] * 2,
+        out_specs=(vmem, vmem, vmem),
         scratch_shapes=[
+            pltpu.VMEM((parts, 2, depth, block, 256), BF16),
+            pltpu.VMEM(fields.shape, BF16),
+            pltpu.VMEM(cotangent.shape, BF16),
+            pltpu.VMEM((1, tokens), jnp.int32),
+            pltpu.VMEM(reward_masks.shape, jnp.int32),
+            pltpu.VMEM((1, cat_weight.shape[0]), F32),
+            pltpu.VMEM(qkv_weight.shape, BF16),
+            pltpu.VMEM(out_weight.shape, BF16),
+            dma((7,)),
             pltpu.VMEM((spread, slots, 2 * channels), BF16),
             pltpu.VMEM((2, spread, slots, 2 * channels), BF16),
             pltpu.VMEM((tokens, width), BF16),
@@ -444,7 +531,7 @@
             dma((parts, depth)), dma((parts, depth)),
         ],
         compiler_params=pltpu.CompilerParams(
-            collective_id=0, has_side_effects=True, vmem_limit_bytes=48 * 1024 * 1024
+            collective_id=0, has_side_effects=True, vmem_limit_bytes=63 * 1024 * 1024
         ),
         cost_estimate=pl.CostEstimate(
             flops=2_000_000_000, bytes_accessed=8_000_000, transcendentals=300_000
@@ -459,10 +546,7 @@
         qkv_weight,
         out_weight,
     )
-    sums = sums.reshape(4, 512, 256)
-    grad_qkv = sums[:3].astype(F32)
-    grad_out = jnp.concatenate([sums[3, :256], sums[3, 256:]], axis=1).astype(F32)
-    return grad_fields, grad_qkv, grad_out
+    return grad_fields, grad_qkv.astype(F32), grad_out.astype(F32)
 
 
 def solution(mesh):

time: 71.2 us -> 62 us (0.87)
  the two profiles are of different devices: /device:TPU:26 before, /device:TPU:0 now
where the time goes in v2:
time: 62 us; the launch traced here: 61.8 us
  Pallas kernels  57.2 us (92%)
  other arithmetic  3.31 us (5%)
  local copies, waits for them, and re-layouts  0.66 us (1%)
  between operations  0.66 us (1%)
    pallas_call x1, Pallas kernels, shards(): pl.pallas_call(functools.partial(kernel, spread), out_shape=(jax.ShapeDty...  57.2 us
    convert_element_type x2, other arithmetic, shards(): return (grad_fields, grad_qkv.astype(F32), grad_out.astype(F32))  3.31 us

profile of v2, /device:TPU:0, one launch (start us, length us, event | category | flops | bytes accessed | tf_op | source)
XLA Modules:
  0.0 61.8 jit_solution(18085094499674355783)
XLA Ops:
  0.6 57.2 %shard_map.103 = (bf16[256,256]{1,0:T(8,128)(2,1)}, bf16[3,512,256]{2,1,0:T(8,128)(2,1)}, bf16[256,512]{1,0:T(8,128)(2,1)}) custom-call(bf16[256,256]{1,0:T(8,128)(2,1)} %fields_hbm.1, bf16[256,256]{1,0:T(8,128)(2,1)} %cotangent_hbm.1, s32[1,256]{1,0:T(1,128)} %bitcast.3, s32[6,256]{1,0:T(8,128)} %masks_hbm.1, f32[1,512]{1,0:T(1,128)} %bitcast.2, ...), custom_call_target="tpu_custom_call" | custom-call | flops 2000000000 | bytes 8000000 | tf_op jit(solution)/shard_map/pallas_call | solution.py:494
  57.8 0.0 copy-start
  57.9 0.0 copy-start.1
  57.9 2.5 %convert_element_type.6 = f32[3,512,256]{2,1,0:T(8,128)} convert(bf16[3,512,256]{2,1,0:T(8,128)(2,1)} %get-tuple-element.7) | non-fusion elementwise | flops 393216 | bytes 2359296 | tf_op jit(solution)/shard_map/convert_element_type | solution.py:549
  60.3 0.0 copy-done
  60.3 0.9 %convert_element_type.7 = f32[256,512]{1,0:T(8,128)} convert(bf16[256,512]{1,0:T(8,128)(2,1)S(1)} %copy-done) | non-fusion elementwise | flops 131072 | bytes 786432 | tf_op jit(solution)/shard_map/convert_element_type | solution.py:549
  61.2 0.0 copy-done.1
  61.2 0.7 %copy.12 = bf16[256,256]{1,0:T(8,128)(2,1)} copy(bf16[256,256]{1,0:T(8,128)(2,1)S(1)} %copy-done.1) | data formatting | bytes 262144
Async XLA Ops:
  57.8 2.5 %copy-start = (bf16[256,512]{1,0:T(8,128)(2,1)S(1)}, bf16[256,512]{1,0:T(8,128)(2,1)}, u32[]{:S(2)}) copy-start(bf16[256,512]{1,0:T(8,128)(2,1)} %get-tuple-element.8) | copy-start | bytes 786436
  57.9 3.3 %copy-start.1 = (bf16[256,256]{1,0:T(8,128)(2,1)S(1)}, bf16[256,256]{1,0:T(8,128)(2,1)}, u32[]{:S(2)}) copy-start(bf16[256,256]{1,0:T(8,128)(2,1)} %get-tuple-element.12) | copy-start | bytes 393220

commit v3 on v2

--- a/solution.py
+++ b/solution.py
@@ -61,7 +61,9 @@
 def split_sum(values, ones):
     high = values.astype(BF16)
     low = (values - high.astype(F32)).astype(BF16)
-    return nn(high, ones) + nn(low, ones)
+    rows = values.shape[0]
+    both = nn(jnp.concatenate([high, low], axis=0), ones)
+    return both[:rows] + both[rows:]
 
 
 def attend(q, k, v, g):
@@ -138,6 +140,8 @@
     terms,
     from_x,
     pair,
+    from_w,
+    quad,
     from_z,
     stack,
     in_send,
@@ -150,10 +154,14 @@
     bk_recv,
     x_send,
     x_recv,
+    w_send,
+    w_recv,
     z_send,
     z_recv,
     gz_send,
     gz_recv,
+    gw_send,
+    gw_recv,
     gx_send,
     gx_recv,
 ):
@@ -175,10 +183,12 @@
     ch = lax.axis_index("ch")
     x, z = lax.rem(me, 2), me // 2
     partner = 2 * z + 1 - x
+    zl, zh = lax.rem(z, 2), z // 2
+    beside = 2 * (2 * zh + 1 - zl) + x
     tokens, channels = fields.shape
     rows = tokens // spread
     slots = send.shape[1]
-    parts, _, depth, block, _ = terms.shape
+    parts, _, _, depth, block, _ = terms.shape
 
     def remote(src, dst, send_sem, recv_sem, where):
         return pltpu.make_async_remote_copy(
@@ -279,35 +289,47 @@
     def store_terms(index, value):
         value = value.astype(BF16)
         if parts == 4:
-            terms[index] = value.reshape(2, depth, block, 256)
+            terms[index] = value.reshape(2, 2, depth, block, 256)
         else:
-            half = depth // 2
-            first = (index % 2) * half
-            terms[0, index // 2, first:first + half] = value.reshape(half, block, 256)
+            terms[0, index // 2, index % 2] = value.reshape(depth, block, 256)
 
     def part_rows(ref, index):
         if parts == 4:
             return ref[index].reshape(512, 256)
-        first = (index % 2) * (depth // 2)
-        return ref[0, index // 2, first:first + depth // 2].reshape(512, 256)
+        return ref[0, index // 2, index % 2].reshape(512, 256)
+
+    def to_beside(part):
+        return remote(
+            pair.at[part, 1 - zl], from_w.at[part], w_send.at[part], w_recv.at[part],
+            {"tok": beside},
+        )
+
+    def z_peer(step):
+        there = lax.rem(zh + step, depth)
+        return there, {"tok": 2 * (2 * there + zl) + x}
 
     def to_z(part, step):
-        there = lax.rem(z + step, depth)
-        return remote(
-            pair.at[part, there], from_z.at[part, z],
-            z_send.at[part, there], z_recv.at[part, z], {"tok": 2 * there + x},
+        there, where = z_peer(step)
+        return remote(
+            quad.at[part, there], from_z.at[part, zh],
+            z_send.at[part, there], z_recv.at[part, zh], where,
         )
 
     def from_z_peer(part, step):
-        there = lax.rem(z + step, depth)
+        there, where = z_peer(step)
         return there, remote(
-            pair.at[part, there], from_z.at[part, there],
-            z_send.at[part, there], z_recv.at[part, there], {"tok": 2 * there + x},
+            quad.at[part, there], from_z.at[part, there],
+            z_send.at[part, there], z_recv.at[part, there], where,
         )
 
     def pair_up(part):
         to_partner(part).wait_recv()
         pair[part] = (terms[part, x].astype(F32) + from_x[part].astype(F32)).astype(BF16)
+        to_beside(part).start()
+
+    def quad_up(part):
+        to_beside(part).wait_recv()
+        quad[part] = (pair[part, zl].astype(F32) + from_w[part].astype(F32)).astype(BF16)
         repeat(1, depth, lambda step: to_z(part, step).start())
 
     turned = normed.astype(F32).T.astype(BF16)
@@ -344,7 +366,11 @@
     dense_copy = remote(dense_send, dense_got, de_send, de_recv, {"ch": 1 - ch})
     dense_copy.start()
 
-    pair_up(1 if parts == 4 else 0)
+    if parts == 4:
+        quad_up(0)
+        pair_up(1)
+    else:
+        pair_up(0)
 
     dense_copy.wait()
     dense = dense_send[...].astype(F32) + dense_got[...].astype(F32)
@@ -375,39 +401,33 @@
     back_got[me] = back_send[me]
 
     def share_z(part, step):
-        there = lax.rem(z + step, depth)
-        return remote(
-            sums.at[part, x, z], sums.at[part, x, z],
-            gz_send.at[part, there], gz_recv.at[part, z], {"tok": 2 * there + x},
-        )
+        there, where = z_peer(step)
+        mine = sums.at[part, x, zl, zh]
+        return remote(mine, mine, gz_send.at[part, there], gz_recv.at[part, zh], where)
 
     def shared_z(part, step):
-        there = lax.rem(z + step, depth)
+        there, where = z_peer(step)
+        other = sums.at[part, x, zl, there]
         return there, remote(
-            sums.at[part, x, there], sums.at[part, x, there],
-            gz_send.at[part, there], gz_recv.at[part, there], {"tok": 2 * there + x},
-        )
-
-    def share_x(part, there):
-        return remote(
-            sums.at[part, x, there], sums.at[part, x, there],
-            gx_send.at[part, there], gx_recv.at[part, there], {"tok": partner},
-        )
-
-    def shared_x(part, there):
-        return remote(
-            sums.at[part, 1 - x, there], sums.at[part, 1 - x, there],
-            gx_send.at[part, there], gx_recv.at[part, there], {"tok": partner},
-        )
-
-    def go_on(part, step):
-        there, copy = shared_z(part, step)
-        copy.wait_recv()
-        share_x(part, there).start()
+            other, other, gz_send.at[part, there], gz_recv.at[part, there], where
+        )
+
+    def share_w(part, there, low_z):
+        held = sums.at[part, x, low_z, there]
+        return remote(
+            held, held, gw_send.at[part, there], gw_recv.at[part, there], {"tok": beside}
+        )
+
+    def share_x(part, there, low_z, of_x):
+        held = sums.at[part, of_x, low_z, there]
+        return remote(
+            held, held, gx_send.at[part, low_z, there], gx_recv.at[part, low_z, there],
+            {"tok": partner},
+        )
 
     def finish(part):
         if depth <= 9:
-            total = pair[part, z].astype(F32)
+            total = quad[part, zh].astype(F32)
             for step in range(1, depth):
                 there, copy = from_z_peer(part, step)
                 copy.wait_recv()
@@ -418,19 +438,34 @@
                 copy.wait_recv()
                 return total + from_z[part, there].astype(F32)
 
-            total = lax.fori_loop(1, depth, add, pair[part, z].astype(F32))
-        sums[part, x, z] = total.astype(BF16)
+            total = lax.fori_loop(1, depth, add, quad[part, zh].astype(F32))
+        sums[part, x, zl, zh] = total.astype(BF16)
         repeat(1, depth, lambda step: share_z(part, step).start())
-        share_x(part, z).start()
+        share_w(part, zh, zl).start()
+        share_x(part, zh, zl, x).start()
+
+    def go_z(part):
+        def go_on(step):
+            there, copy = shared_z(part, step)
+            copy.wait_recv()
+            share_w(part, there, zl).start()
+            share_x(part, there, zl, x).start()
+
+        repeat(1, depth, go_on)
+
+    def go_w(part):
+        def go_on(step):
+            there = lax.rem(zh + step, depth)
+            share_w(part, there, 1 - zl).wait_recv()
+            share_x(part, there, 1 - zl, x).start()
+
+        repeat(0, depth, go_on)
 
     def restore():
         repeat(1, spread, lambda k: take_back(k).wait_recv())
         order_back = spread_matrix(tokens, spread, rows, slots, True)
         restored = nn(order_back, back_got[...].reshape(spread * slots, channels))
         out_fields[...] = restored.astype(BF16)
-
-    def pass_over(part):
-        repeat(1, depth, lambda step: go_on(part, step))
 
     def place_terms(index):
         block_rows = part_rows(sums, index)
@@ -445,23 +480,33 @@
                 out_out[cols, j * half:(j + 1) * half] = block_rows[j * half:(j + 1) * half, half:]
 
     if parts == 4:
+        quad_up(1)
+        pair_up(2)
         finish(0)
-        pair_up(2)
+        quad_up(2)
+        pair_up(3)
         finish(1)
-        pass_over(0)
-        pair_up(3)
+        go_z(0)
+        quad_up(3)
         finish(2)
-        pass_over(1)
+        go_w(0)
+        go_z(1)
+        finish(3)
+        go_w(1)
+        go_z(2)
         restore()
-        finish(3)
-        pass_over(2)
-        pass_over(3)
+        go_z(3)
+        go_w(2)
+        go_w(3)
     else:
+        quad_up(0)
         finish(0)
         restore()
-        pass_over(0)
+        go_z(0)
+        go_w(0)
     for part in range(parts):
-        repeat(0, depth, lambda there: shared_x(part, there).wait_recv())
+        for low_z in range(2):
+            repeat(0, depth, lambda there: share_x(part, there, low_z, 1 - x).wait_recv())
         if parts == 4:
             place_terms(part)
     if parts == 1:
@@ -473,16 +518,45 @@
     repeat(1, spread, lambda k: give_back(k).wait_send())
     for part in range(parts):
         to_partner(part).wait_send()
+        to_beside(part).wait_send()
         repeat(1, depth, lambda step: to_z(part, step).wait_send())
         repeat(1, depth, lambda step: share_z(part, step).wait_send())
-        repeat(0, depth, lambda there: share_x(part, there).wait_send())
+        repeat(0, depth, lambda there: share_w(part, there, zl).wait_send())
+        for low_z in range(2):
+            repeat(0, depth, lambda there: share_x(part, there, low_z, x).wait_send())
+
+
+def widen_kernel(fields, qkv, out, fields_wide, qkv_wide, out_wide):
+    fields_wide[...] = fields[...]
+    qkv_wide[...] = qkv[...].astype(F32)
+    out_wide[...] = out[...].astype(F32)
+
+
+def widen(fields, qkv, out):
+    steps = 1
+    flat = qkv.reshape(-1, qkv.shape[2])
+    arrays = (fields, flat, out)
+    specs = [pl.BlockSpec((a.shape[0] // steps, a.shape[1]), lambda i: (i, 0)) for a in arrays]
+    fields, flat, out = pl.pallas_call(
+        widen_kernel,
+        grid=(steps,),
+        out_shape=(
+            jax.ShapeDtypeStruct(fields.shape, BF16),
+            jax.ShapeDtypeStruct(flat.shape, F32),
+            jax.ShapeDtypeStruct(out.shape, F32),
+        ),
+        in_specs=specs,
+        out_specs=specs,
+        compiler_params=pltpu.CompilerParams(vmem_limit_bytes=63 * 1024 * 1024),
+    )(*arrays)
+    return fields, flat.reshape(qkv.shape), out
 
 
 def shards(fields, cotangent, labels, reward_masks, cat_weight, var_weight, qkv_weight, out_weight):
     tokens, channels = fields.shape
     spread = lax.axis_size("tok")
     slots = max(tokens // spread, 16)
-    depth = spread // 2
+    depth = spread // 4
     width = qkv_weight.shape[1]
     total = 2048
     parts = 4 if total // (4 * spread) >= 16 else 1
@@ -501,7 +575,7 @@
         in_specs=[hbm] * 5 + [smem] + [hbm] * 2,
         out_specs=(vmem, vmem, vmem),
         scratch_shapes=[
-            pltpu.VMEM((parts, 2, depth, block, 256), BF16),
+            pltpu.VMEM((parts, 2, 2, depth, block, 256), BF16),
             pltpu.VMEM(fields.shape, BF16),
             pltpu.VMEM(cotangent.shape, BF16),
             pltpu.VMEM((1, tokens), jnp.int32),
@@ -516,6 +590,8 @@
             pltpu.VMEM((tokens, width), BF16),
             pltpu.VMEM((spread, slots, channels), BF16),
             pltpu.VMEM((spread, slots, channels), BF16),
+            pltpu.VMEM((parts, 2, 2, depth, block, 256), BF16),
+            pltpu.VMEM((parts, 2, depth, block, 256), BF16),
             pltpu.VMEM((parts, 2, depth, block, 256), BF16),
             pltpu.VMEM((parts, depth, block, 256), BF16),
             pltpu.VMEM((parts, depth, block, 256), BF16),
@@ -526,9 +602,11 @@
             dma, dma,
             dma((spread,)), dma((spread,)),
             dma((parts,)), dma((parts,)),
+            dma((parts,)), dma((parts,)),
             dma((parts, depth)), dma((parts, depth)),
             dma((parts, depth)), dma((parts, depth)),
             dma((parts, depth)), dma((parts, depth)),
+            dma((parts, 2, depth)), dma((parts, 2, depth)),
         ],
         compiler_params=pltpu.CompilerParams(
             collective_id=0, has_side_effects=True, vmem_limit_bytes=63 * 1024 * 1024
@@ -546,7 +624,7 @@
         qkv_weight,
         out_weight,
     )
-    return grad_fields, grad_qkv.astype(F32), grad_out.astype(F32)
+    return widen(grad_fields, grad_qkv, grad_out)
 
 
 def solution(mesh):

time: 62 us -> 59.6 us (0.961)
  other arithmetic: 3.31 us -> 0 us
  Pallas kernels: 57.2 us -> 58.8 us
  local copies, waits for them, and re-layouts: 0.66 us -> 0 us
    convert_element_type x2 -> x0, other arithmetic: 3.31 us -> none  [shards(): return (grad_fields, grad_qkv.astype(F32), grad_out.astype(F32))]
    pallas_call x0 -> x1, Pallas kernels: none -> 2.67 us  [widen(): pl.pallas_call(widen_kernel, grid=(steps,), out_shape=(jax.ShapeDtypeStru...]
    pallas_call x1, Pallas kernels: 57.2 us -> 56.1 us  [shards(): pl.pallas_call(functools.partial(kernel, spread), out_shape=(jax.ShapeDty...]
    unnamed x5 -> x0, local copies, waits for them, and re-layouts: 0.66 us -> none
where the time goes in v3:
time: 59.6 us; the launch traced here: 59.4 us
  Pallas kernels  58.8 us (99%)
  between operations  0.64 us (1%)
    pallas_call x1, Pallas kernels, shards(): pl.pallas_call(functools.partial(kernel, spread), out_shape=(jax.ShapeDty...  56.1 us
    pallas_call x1, Pallas kernels, widen(): pl.pallas_call(widen_kernel, grid=(steps,), out_shape=(jax.ShapeDtypeStru...  2.67 us

profile of v3, /device:TPU:0, one launch (start us, length us, event | category | flops | bytes accessed | tf_op | source)
XLA Modules:
  0.0 59.4 jit_solution(17890169883182771242)
XLA Ops:
  0.6 56.1 %shard_map.103 = (bf16[256,256]{1,0:T(8,128)(2,1)}, bf16[3,512,256]{2,1,0:T(8,128)(2,1)}, bf16[256,512]{1,0:T(8,128)(2,1)}) custom-call(bf16[256,256]{1,0:T(8,128)(2,1)} %fields_hbm.1, bf16[256,256]{1,0:T(8,128)(2,1)} %cotangent_hbm.1, s32[1,256]{1,0:T(1,128)} %bitcast.7, s32[6,256]{1,0:T(8,128)} %masks_hbm.1, f32[1,512]{1,0:T(1,128)} %bitcast.6, ...), custom_call_target="tpu_custom_call" | custom-call | flops 2000000000 | bytes 8000000 | tf_op jit(solution)/shard_map/pallas_call | solution.py:568
  56.7 2.7 %shard_map.104 = (bf16[256,256]{1,0:T(8,128)(2,1)}, f32[1536,256]{1,0:T(8,128)}, f32[256,512]{1,0:T(8,128)}) custom-call(bf16[256,256]{1,0:T(8,128)(2,1)} %get-tuple-element.9.fields, bf16[1536,256]{1,0:T(8,128)(2,1)} %bitcast.4, bf16[256,512]{1,0:T(8,128)(2,1)} %get-tuple-element.11.out), custom_call_target="tpu_custom_call" | custom-call | tf_op jit(solution)/shard_map/pallas_call | solution.py:540

commit v4 on v3

--- a/solution.py
+++ b/solution.py
@@ -350,6 +350,8 @@
         store_terms(2 * h, nn(turned, both))
         if parts == 4:
             to_partner(2 * h).start()
+            if h == 1:
+                pair_up(1)
         out_term = tn(stack[0, :, cols], grad_full)
         out_term = jnp.concatenate(
             [out_term[:, j * half:(j + 1) * half] for j in range(4)], axis=0
@@ -368,7 +370,6 @@
 
     if parts == 4:
         quad_up(0)
-        pair_up(1)
     else:
         pair_up(0)
 
@@ -533,7 +534,7 @@
 
 
 def widen(fields, qkv, out):
-    steps = 1
+    steps = 2
     flat = qkv.reshape(-1, qkv.shape[2])
     arrays = (fields, flat, out)
     specs = [pl.BlockSpec((a.shape[0] // steps, a.shape[1]), lambda i: (i, 0)) for a in arrays]

time: 59.6 us -> 58.8 us (0.987)
  Pallas kernels: 58.8 us -> 58 us
where the time goes in v4:
time: 58.8 us; the launch traced here: 58.7 us
  Pallas kernels  58 us (99%)
  between operations  0.64 us (1%)
    pallas_call x1, Pallas kernels, shards(): pl.pallas_call(functools.partial(kernel, spread), out_shape=(jax.ShapeDty...  55.5 us
    pallas_call x1, Pallas kernels, widen(): pl.pallas_call(widen_kernel, grid=(steps,), out_shape=(jax.ShapeDtypeStru...  2.48 us

profile of v4, /device:TPU:0, one launch (start us, length us, event | category | flops | bytes accessed | tf_op | source)
XLA Modules:
  0.0 58.7 jit_solution(7203553543327149551)
XLA Ops:
  0.6 55.5 %shard_map.103 = (bf16[256,256]{1,0:T(8,128)(2,1)}, bf16[3,512,256]{2,1,0:T(8,128)(2,1)}, bf16[256,512]{1,0:T(8,128)(2,1)}) custom-call(bf16[256,256]{1,0:T(8,128)(2,1)} %fields_hbm.1, bf16[256,256]{1,0:T(8,128)(2,1)} %cotangent_hbm.1, s32[1,256]{1,0:T(1,128)} %bitcast.7, s32[6,256]{1,0:T(8,128)} %masks_hbm.1, f32[1,512]{1,0:T(1,128)} %bitcast.6, ...), custom_call_target="tpu_custom_call" | custom-call | flops 2000000000 | bytes 8000000 | tf_op jit(solution)/shard_map/pallas_call | solution.py:569
  56.2 2.5 %shard_map.104 = (bf16[256,256]{1,0:T(8,128)(2,1)}, f32[1536,256]{1,0:T(8,128)}, f32[256,512]{1,0:T(8,128)}) custom-call(bf16[256,256]{1,0:T(8,128)(2,1)} %get-tuple-element.9.fields, bf16[1536,256]{1,0:T(8,128)(2,1)} %bitcast.4, bf16[256,512]{1,0:T(8,128)(2,1)} %get-tuple-element.11.out), custom_call_target="tpu_custom_call" | custom-call | tf_op jit(solution)/shard_map/pallas_call | solution.py:541
